TPU v7x, 32 devices: a whole 2x2x4 slice. The times are simulated.
32 devices in a mesh: frame: 8 (over z, x), row: 4 (over y, core).
Axes of the slice: x: 2, y: 2, z: 4, core: 2. Of those that a mesh axis runs over, the one named last changes fastest.
Arguments:
- tokens: bfloat16 [8, 1024, 512], P('frame', 'row'), may hold values from -15 to 15
- norm_spatial: float32 [512], replicated, may hold values from 0.25 to 1.75
- w_spatial: bfloat16 [512, 1536], replicated, may hold values from -10 to 10
- w_spatial_out: bfloat16 [512, 512], replicated, may hold values from -0.25 to 0.25
- norm_temporal: float32 [512], replicated, may hold values from 0.25 to 1.75
- w_temporal: bfloat16 [512, 1536], replicated, may hold values from -10 to 10
- w_temporal_out: bfloat16 [512, 512], replicated, may hold values from -0.25 to 0.25
Outputs:
- mixed: bfloat16 [8, 1024, 512], P('frame', 'row')
All inputs are finite; a program needn't handle non-finite values.
Results may differ from a plain program's by a relative error of at most 0.01.
The roundings to bfloat16 on the way count: a program that leaves them out, or rounds other values in their place, can miss the bound.
Values may be sent and summed in bfloat16 or wider, within the bound.
A program may use at most 64 MiB of HBM per device.

v0:
```python
import math

import jax
import jax.numpy as jnp
from jax import lax
from jax.sharding import PartitionSpec as P

HEADS = 8


def layer_norm(rows, gain):
    mean = jnp.mean(rows, axis=-1, keepdims=True)
    centred = rows - mean
    spread = jnp.mean(centred * centred, axis=-1, keepdims=True)
    return centred * lax.rsqrt(spread + 1e-05) * gain


def fold_keys(state, keys, values, query, scale):
    count = keys.shape[0]
    block = math.gcd(count, 512)

    def one_block(index, carry):
        peak, total, summed = carry
        key_rows = lax.dynamic_slice_in_dim(keys, index * block, block, 0)
        value_rows = lax.dynamic_slice_in_dim(values, index * block, block, 0)
        scores = (
            jnp.einsum("qhe,khe->hqk", query, key_rows, preferred_element_type=jnp.float32) * scale
        )
        fresh = jnp.maximum(peak, jnp.max(scores, axis=2))
        fade = jnp.exp(peak - fresh)
        weights = jnp.exp(scores - fresh[:, :, None])
        total = total * fade + jnp.sum(weights, axis=2)
        summed = summed * fade[:, :, None] + jnp.einsum(
            "hqk,khe->hqe",
            weights.astype(jnp.bfloat16),
            value_rows,
            preferred_element_type=jnp.float32,
        )
        return (fresh, total, summed)

    return lax.fori_loop(0, count // block, one_block, state)


def attend_cells(block_qkv):
    frames, cells = (block_qkv.shape[0], block_qkv.shape[1])
    width = block_qkv.shape[2] // 3
    size = width // HEADS
    scale = 1.0 / math.sqrt(size)
    query = block_qkv[:, :, :width].reshape(frames, cells, HEADS, size)
    keys = block_qkv[:, :, width : 2 * width].reshape(frames, cells, HEADS, size)
    values = block_qkv[:, :, 2 * width :].reshape(frames, cells, HEADS, size)
    scores = jnp.einsum("fche,gche->chfg", query, keys, preferred_element_type=jnp.float32) * scale
    later = jnp.arange(frames)[:, None] >= jnp.arange(frames)[None, :]
    scores = jnp.where(later, scores, -1e30)
    peak = jnp.max(scores, axis=3, keepdims=True)
    weights = jnp.exp(scores - peak)
    total = jnp.sum(weights, axis=3)
    summed = jnp.einsum(
        "chfg,gche->fche", weights.astype(jnp.bfloat16), values, preferred_element_type=jnp.float32
    )
    context = summed / jnp.transpose(total, (2, 0, 1))[..., None]
    return context.reshape(frames, cells, width).astype(jnp.bfloat16)


def owner_attend(block_qkv):
    frames, single, cells, triple = block_qkv.shape
    result = attend_cells(block_qkv.reshape(frames, single * cells, triple))
    return result.reshape(frames, single, cells, triple // 3)


def shards(
    tokens, norm_spatial, w_spatial, w_spatial_out, norm_temporal, w_temporal, w_temporal_out
):
    frames_here, rows, width = tokens.shape
    size = width // HEADS
    scale = 1.0 / math.sqrt(size)
    count = frames_here * rows
    resid = tokens.reshape(count, width).astype(jnp.float32)
    normed = layer_norm(resid, norm_spatial).astype(jnp.bfloat16)
    query_flat = jnp.dot(normed, w_spatial[:, :width], preferred_element_type=jnp.float32).astype(
        jnp.bfloat16
    )
    query = query_flat.reshape(count, HEADS, size)
    initial = (
        jnp.full((HEADS, count), -1e30, jnp.float32),
        jnp.zeros((HEADS, count), jnp.float32),
        jnp.zeros((HEADS, count, size), jnp.float32),
    )
    pairs = jnp.dot(normed, w_spatial[:, width:], preferred_element_type=jnp.float32).astype(
        jnp.bfloat16
    )
    piece = lax.all_gather(pairs, "row", axis=0, tiled=True)
    length = piece.shape[0]
    peak, total, summed = fold_keys(
        initial,
        piece[:, :width].reshape(length, HEADS, size),
        piece[:, width:].reshape(length, HEADS, size),
        query,
        scale,
    )
    context = summed / total[:, :, None]
    context = jnp.transpose(context, (1, 0, 2)).reshape(count, width).astype(jnp.bfloat16)
    after = resid + jnp.dot(context, w_spatial_out, preferred_element_type=jnp.float32)
    second = layer_norm(after, norm_temporal).astype(jnp.bfloat16)
    owners = lax.axis_size("frame")
    share = rows // owners
    qkv_t = jnp.dot(second, w_temporal, preferred_element_type=jnp.float32).astype(jnp.bfloat16)
    qkv_t = qkv_t.reshape(frames_here, owners, share, 3 * width)
    gathered = owner_attend(lax.all_to_all(qkv_t, "frame", split_axis=1, concat_axis=0, tiled=True))
    returned = lax.all_to_all(gathered, "frame", split_axis=0, concat_axis=1, tiled=True)
    mixed = after + jnp.dot(
        returned.reshape(count, width), w_temporal_out, preferred_element_type=jnp.float32
    )
    return mixed.reshape(frames_here, rows, width).astype(jnp.bfloat16)


def solution(mesh):
    in_specs = (P("frame", "row", None), P(), P(), P(), P(), P(), P())
    out_specs = P("frame", "row", None)
    return jax.shard_map(shards, mesh=mesh, in_specs=in_specs, out_specs=out_specs, check_vma=False)
```

profile of v0, /device:TPU:0, one launch (start us, length us, event | category | flops | bytes accessed | tf_op | source)
XLA Modules:
  0.0 118.6 jit_solution(11196386600482184982)
XLA Ops:
  6.5 1.2 convert_reduce_fusion
  7.7 1.2 fusion.28
  8.9 2.6 %convolution_convert_fusion.1 = bf16[256,1024]{1,0:T(8,128)(2,1)} fusion(bf16[512,1536]{1,0:T(8,128)(2,1)} %param.11, bf16[1,256,512]{2,1,0:T(8,128)(2,1)} %param.9, f32[512]{0:T(512)} %param.10, f32[256]{0:T(256)S(1)} %add_rsqrt_fusion.1, f32[256]{0:T(256)S(1)} %broadcast_multiply_fusion.1), kind=kOutput, calls=%fused_computation.25 | convolution fusion | flops 269352960 | bytes 1839104 | tf_op jit(solution)/shard_map/dot_general | solution.py:89
  11.6 1.5 %convolution_convert_fusion.2 = bf16[256,512]{1,0:T(8,128)(2,1)S(1)} fusion(bf16[512,1536]{1,0:T(8,128)(2,1)} %param.11, bf16[1,256,512]{2,1,0:T(8,128)(2,1)} %param.9, f32[512]{0:T(512)} %param.10, f32[256]{0:T(256)S(1)} %add_rsqrt_fusion.1, f32[256]{0:T(256)S(1)} %broadcast_multiply_fusion.1), kind=kOutput, calls=%fused_computation.30 | convolution fusion | flops 135004160 | bytes 1052672 | tf_op jit(solution)/shard_map/dot_general | solution.py:80
  13.2 23.8 %all-gather.2.cloned.1.call-done = bf16[1024,1024]{1,0:T(8,128)(2,1)} async-done(((bf16[256,1024]{1,0:T(8,128)(2,1)}), bf16[1024,1024]{1,0:T(8,128)(2,1)}) %all-gather.2.cloned.1.call-update) | async-done | bytes 2097168 | tf_op jit(solution)/shard_map/all_gather | solution.py:92
  37.0 3.0 %fusion.42 = (bf16[1024,512]{1,0:T(8,128)(2,1)}, bf16[1024,512]{1,0:T(8,128)(2,1)}) fusion(bf16[1024,1024]{1,0:T(8,128)(2,1)} %all-gather.2.cloned.1.call-done), kind=kLoop, calls=%fused_computation.60 | loop fusion | bytes 4194304 | tf_op jit(solution)/shard_map/slice | solution.py:97
  40.0 1.5 %copy.23 = bf16[1024,512]{0,1:T(8,128)(2,1)S(1)} copy(bf16[1024,512]{1,0:T(8,128)(2,1)} %get-tuple-element.182) | data formatting | bytes 2097152 | tf_op jit(solution)/shard_map/slice | solution.py:96
  41.5 2.3 %copy.25 = bf16[1024,512]{0,1:T(8,128)(2,1)} copy(bf16[1024,512]{1,0:T(8,128)(2,1)} %get-tuple-element.181) | data formatting | bytes 2097152 | tf_op jit(solution)/shard_map/slice | solution.py:97
  43.8 16.3 %while.18 = (s32[]{:T(128)}, f32[8,256]{1,0:T(8,128)S(1)}, f32[8,256]{1,0:T(8,128)S(1)}, f32[8,256,64]{1,2,0:T(8,128)S(1)}, bf16[1024,8,64]{0,2,1:T(8,128)(2,1)S...) while((s32[]{:T(128)}, f32[8,256]{1,0:T(8,128)S(1)}, ...), condition=%wide.region_5.0_spmd.clone, body=%wide.region_2.0_spmd.clone.sunk | while | flops 277227520 | bytes 31850696 | solution.py:41
  43.8 2.7 %bitcast_reduce_fusion.2 = (f32[8,256]{1,0:T(8,128)S(1)}, f32[8,512,256]{2,1,0:T(8,128)}) fusion(bf16[256,8,64]{0,2,1:T(8,128)(2,1)S(1)} %get-tuple-element.268, bf16[1024,8,64]{0,2,1:T(8,128)(2,1)S(1)} %get-tuple-element.267, s32[]{:T(128)S(6)} %select_n.16), kind=kOutput, calls=%fused_computation.1.clone.1 | convolution fusion | flops 136312832 | bytes 4988932 | tf_op jit(solution)/shard_map/while/body/eval_jaxpr/qhe,khe->hqk/dot_general | solution.py:27
  46.5 3.0 %fusion.61 = f32[8,256]{1,0:T(8,128)S(1)} fusion(f32[8,512,256]{2,1,0:T(8,128)} %get-tuple-element.238, f32[8,256]{1,0:T(8,128)S(1)} %select_maximum_fusion.2), kind=kLoop, calls=%fused_computation.4.clone.1 | loop fusion | flops 3143680 | bytes 4210688 | tf_op jit(solution)/shard_map/while/body/eval_jaxpr/reduce_sum | solution.py:32
  49.9 2.0 %fusion.63 = f32[8,256,64]{1,2,0:T(8,128)S(1)} fusion(f32[8,512,256]{2,1,0:T(8,128)S(1)} %copy-done.1, f32[8,256]{1,0:T(8,128)S(1)} %select_maximum_fusion.2, f32[8,256,64]{1,2,0:T(8,128)S(1)} %get-tuple-element.255, bf16[1024,8,64]{0,2,1:T(8,128)(2,1)} %get-tuple-element.269, s32[]{:T(128)S(6)} %select_n.16, f32[8,256]{1,0:T(8,128)S(1)} %get-tuple-element.240, ...), kind=kOutput, calls=%fused_computation.8.clone.1 | convolution fusion | flops 137756672 | bytes 5783557 | tf_op jit(solution)/shard_map/while/body/eval_jaxpr/hqk,khe->hqe/dot_general | solution.py:33
  51.9 2.7 %bitcast_reduce_fusion.2 = (f32[8,256]{1,0:T(8,128)S(1)}, f32[8,512,256]{2,1,0:T(8,128)}) fusion(bf16[256,8,64]{0,2,1:T(8,128)(2,1)S(1)} %get-tuple-element.268, bf16[1024,8,64]{0,2,1:T(8,128)(2,1)S(1)} %get-tuple-element.267, s32[]{:T(128)S(6)} %select_n.16), kind=kOutput, calls=%fused_computation.1.clone.1 | convolution fusion | flops 136312832 | bytes 4988932 | tf_op jit(solution)/shard_map/while/body/eval_jaxpr/qhe,khe->hqk/dot_general | solution.py:27
  54.6 3.0 %fusion.61 = f32[8,256]{1,0:T(8,128)S(1)} fusion(f32[8,512,256]{2,1,0:T(8,128)} %get-tuple-element.238, f32[8,256]{1,0:T(8,128)S(1)} %select_maximum_fusion.2), kind=kLoop, calls=%fused_computation.4.clone.1 | loop fusion | flops 3143680 | bytes 4210688 | tf_op jit(solution)/shard_map/while/body/eval_jaxpr/reduce_sum | solution.py:32
  58.1 2.0 %fusion.63 = f32[8,256,64]{1,2,0:T(8,128)S(1)} fusion(f32[8,512,256]{2,1,0:T(8,128)S(1)} %copy-done.1, f32[8,256]{1,0:T(8,128)S(1)} %select_maximum_fusion.2, f32[8,256,64]{1,2,0:T(8,128)S(1)} %get-tuple-element.255, bf16[1024,8,64]{0,2,1:T(8,128)(2,1)} %get-tuple-element.269, s32[]{:T(128)S(6)} %select_n.16, f32[8,256]{1,0:T(8,128)S(1)} %get-tuple-element.240, ...), kind=kOutput, calls=%fused_computation.8.clone.1 | convolution fusion | flops 137756672 | bytes 5783557 | tf_op jit(solution)/shard_map/while/body/eval_jaxpr/hqk,khe->hqe/dot_general | solution.py:33
  60.1 1.5 %fusion.44 = (f32[256]{0:T(256)S(1)}, f32[256,512]{1,0:T(8,128)S(1)}) fusion(bf16[256,512]{0,1:T(8,128)(2,1)S(1)} %bitcast.73, bf16[512,512]{1,0:T(8,128)(2,1)} %param.12, bf16[1,256,512]{2,1,0:T(8,128)(2,1)} %param.9), kind=kOutput, calls=%fused_computation.62 | convolution fusion | flops 134610688 | bytes 1573888 | tf_op jit(solution)/shard_map/dot_general | solution.py:103
  61.9 1.5 %convolution_convert_fusion = bf16[256,1536]{1,0:T(8,128)(2,1)} fusion(bf16[512,1536]{1,0:T(8,128)(2,1)S(1)} %copy-done, f32[256,512]{1,0:T(8,128)S(1)} %get-tuple-element.187, f32[512]{0:T(512)S(1)} %copy-done.3, f32[256]{0:T(256)S(1)} %add_rsqrt_fusion, f32[256]{0:T(256)S(1)} %broadcast_multiply_fusion), kind=kOutput, calls=%fused_computation.20 | convolution fusion | flops 403570688 | bytes 2887680 | tf_op jit(solution)/shard_map/dot_general | solution.py:107
  63.4 5.5 %all-to-all-start = ((bf16[1,8,32,1536]{3,2,0,1:T(8,128)(2,1)}), bf16[1,8,32,1536]{3,2,0,1:T(8,128)(2,1)S(1)}, u32[]{:S(2)}, u32[]{:S(2)}) async-start(bf16[1,8,32,1536]{3,2,0,1:T(8,128)(2,1)} %bitcast.71), calls=%async_computation | async-start | bytes 1572864 | tf_op jit(solution)/shard_map/all_to_all | solution.py:109
  68.9 20.5 %all-to-all-done = bf16[1,8,32,1536]{3,2,0,1:T(8,128)(2,1)S(1)} async-done(((bf16[1,8,32,1536]{3,2,0,1:T(8,128)(2,1)}), bf16[1,8,32,1536]{3,2,0,1:T(8,128)(2,1)S(1)}, u32[]{:S(2)}, u32[]{:S(2)}) %all-to-all-start) | async-done | bytes 786464 | tf_op jit(solution)/shard_map/all_to_all | solution.py:109
  90.3 1.3 %reshape.91 = bf16[8,32,8,64]{3,2,1,0:T(8,128)(2,1)S(1)} reshape(bf16[8,32,512]{2,1,0:T(8,128)(2,1)} %get-tuple-element.185) | data formatting | bytes 524288 | tf_op jit(solution)/shard_map/reshape | solution.py:49
  92.6 1.1 reshape.90
  93.7 1.9 %fusion.45 = (f32[32,8,8]{2,1,0:T(8,128)S(1)}, f32[32,8,8,8]{2,3,1,0:T(8,128)S(1)}) fusion(bf16[8,32,8,64]{3,2,1,0:T(8,128)(2,1)} %reshape.92, bf16[8,32,8,64]{3,2,1,0:T(8,128)(2,1)S(1)} %reshape.91, pred[8,8]{0,1:T(8,128)(4,1)S(1)} %iota_compare_fusion), kind=kOutput, calls=%fused_computation.63 | convolution fusion | flops 2144256 | bytes 598080 | tf_op jit(solution)/shard_map/fche,gche->chfg/dot_general | solution.py:52
  96.1 1.8 %fusion.19 = bf16[8,32,8,64]{3,0,2,1:T(8,128)(2,1)S(1)} fusion(f32[32,8,8,8]{2,3,1,0:T(8,128)S(1)} %get-tuple-element.189, bf16[8,32,8,64]{3,2,1,0:T(8,128)(2,1)} %reshape.90, f32[8,32,8]{0,2,1:T(8,128)S(1)} %bitcast.75, f32[32,8,8]{2,1,0:T(8,128)S(1)} %get-tuple-element.188), kind=kOutput, calls=%fused_computation.26 | convolution fusion | flops 2392064 | bytes 606208 | tf_op jit(solution)/shard_map/chfg,gche->fche/dot_general | solution.py:58
  98.2 12.5 %all_to_all.8 = bf16[8,1,32,512]{3,2,1,0:T(8,128)(2,1)S(1)} all-to-all(bf16[8,1,32,512]{3,2,1,0:T(8,128)(2,1)S(1)} %bitcast.72), channel_id=1, replica_groups=mesh['frame'=8,'row'=4] {'frame'}, dimensions={0} | all-to-all | bytes 524288 | tf_op jit(solution)/shard_map/all_to_all | solution.py:110
  (35 shorter events, 5.0 us)
Async XLA Ops:
  6.5 55.4 %copy-start = (bf16[512,1536]{1,0:T(8,128)(2,1)S(1)}, bf16[512,1536]{1,0:T(8,128)(2,1)}, u32[]{:S(2)}) copy-start(bf16[512,1536]{1,0:T(8,128)(2,1)} %param.14) | copy-start | bytes 4718596
  6.5 30.5 %all-gather.2.cloned.1.call-start = ((), (), s32[]{:S(2)}) async-start(), calls=%async_computation.2 | async-start | bytes 2621440 | tf_op jit(solution)/shard_map/all_gather | solution.py:92
  43.8 18.1 %copy-start.3 = (f32[512]{0:T(512)S(1)}, f32[512]{0:T(512)}, u32[]{:S(2)}) copy-start(f32[512]{0:T(512)} %param.13) | copy-start | bytes 6148
  46.5 3.4 %copy-start.1 = (f32[8,512,256]{2,1,0:T(8,128)S(1)}, f32[8,512,256]{2,1,0:T(8,128)}, u32[]{:S(2)}) copy-start(f32[8,512,256]{2,1,0:T(8,128)} %get-tuple-element.238) | copy-start | bytes 12582916 | tf_op jit(solution)/shard_map/while
  54.6 3.4 %copy-start.1 = (f32[8,512,256]{2,1,0:T(8,128)S(1)}, f32[8,512,256]{2,1,0:T(8,128)}, u32[]{:S(2)}) copy-start(f32[8,512,256]{2,1,0:T(8,128)} %get-tuple-element.238) | copy-start | bytes 12582916 | tf_op jit(solution)/shard_map/while
  63.4 26.1 %all-to-all-start = ((bf16[1,8,32,1536]{3,2,0,1:T(8,128)(2,1)}), bf16[1,8,32,1536]{3,2,0,1:T(8,128)(2,1)S(1)}, u32[]{:S(2)}, u32[]{:S(2)}) async-start(bf16[1,8,32,1536]{3,2,0,1:T(8,128)(2,1)} %bitcast.71), calls=%async_computation | async-start | bytes 1572864 | tf_op jit(solution)/shard_map/all_to_all | solution.py:109
  95.6 15.2 %copy-start.2 = (bf16[512,512]{1,0:T(8,128)(2,1)S(1)}, bf16[512,512]{1,0:T(8,128)(2,1)}, u32[]{:S(2)}) copy-start(bf16[512,512]{1,0:T(8,128)(2,1)} %param.15) | copy-start | bytes 1572868
Sparse Core Ops, SparseCore 0:
  11.7 25.2 all-gather.1
where the time goes:
time: 119 us
  waiting for transfers between devices  44.3 us (37%)
  matrix products  21.2 us (18%)
  between operations  13.6 us (11%)
  blocking collectives  12.5 us (11%)
  local copies, waits for them, and re-layouts  12.3 us (10%)
  other arithmetic  9.17 us (8%)
  starting transfers between devices  5.51 us (5%)
    all_gather x1, waiting for transfers between devices, shards(): piece = lax.all_gather(pairs, 'row', axis=0, tiled=True)  23.8 us
    all_to_all x1, waiting for transfers between devices, shards(): lax.all_to_all(qkv_t, 'frame', split_axis=1, concat_axis=0, tiled=True)  20.5 us
    all_to_all x1, blocking collectives, shards(): lax.all_to_all(gathered, 'frame', split_axis=0, concat_axis=1, tiled=True)  12.5 us
    reduce_sum x2, other arithmetic, one_block(): total = total * fade + jnp.sum(weights, axis=2)  6.06 us
    all_to_all x1, starting transfers between devices, shards(): lax.all_to_all(qkv_t, 'frame', split_axis=1, concat_axis=0, tiled=True)  5.51 us
    dot_general x2, matrix products, one_block(): jnp.einsum('qhe,khe->hqk', query, key_rows, preferred_element_type=jnp.fl...  5.39 us
    slice x2, local copies, waits for them, and re-layouts, shards(): piece[:, width:].reshape(length, HEADS, size)  5.26 us
    dot_general x2, matrix products, one_block(): jnp.einsum('hqk,khe->hqe', weights.astype(jnp.bfloat16), value_rows, pref...  3.97 us
  transfers between devices with their start and end apart: 2, of which 2 were waited for; matrix products, arithmetic and copies ran while one was open for 1% of the time, Pallas kernels for 0%

commit v1 on v0

v1 whole, which is shorter than its diff:
```python
import functools
import math

import jax
import jax.numpy as jnp
from jax import lax
from jax.experimental import pallas as pl
from jax.experimental.pallas import tpu as pltpu
from jax.sharding import PartitionSpec as P

HEADS = 8
HEAD = 64
GROUP = 4
HALVES = 2
FACTOR = math.log2(math.e) / math.sqrt(HEAD)
MESH = pl.DeviceIdType.MESH


def layer_norm(rows, gain):
    mean = jnp.mean(rows, axis=-1, keepdims=True)
    centred = rows - mean
    spread = jnp.mean(centred * centred, axis=-1, keepdims=True)
    return centred * lax.rsqrt(spread + 1e-05) * gain


def dot(a, b):
    return jnp.dot(a, b, preferred_element_type=jnp.float32)


def dot_t(a, b):
    return lax.dot_general(a, b, (((1,), (1,)), ((), ())), preferred_element_type=jnp.float32)


def own_lanes(shape, head):
    return lax.div(lax.broadcasted_iota(jnp.int32, shape, 1), jnp.int32(HEAD)) == head


def stack_heads(query):
    wide = query.astype(jnp.float32)
    parts = [jnp.where(own_lanes(query.shape, h), wide, 0.0) for h in range(GROUP)]
    return jnp.concatenate(parts, axis=0).astype(jnp.bfloat16)


def unstack_heads(stacked):
    n = stacked.shape[0] // GROUP
    result = stacked[:n]
    for h in range(1, GROUP):
        part = stacked[h * n : (h + 1) * n]
        result = jnp.where(own_lanes(part.shape, h), part, result)
    return result


def loop(low, high, body):
    if high - low <= 1:
        for i in range(low, high):
            body(i)
    else:
        lax.fori_loop(low, high, lambda i, c: (body(i), c)[1], 0)


def rows_of(block):
    owners, share, width = block.shape
    if share % 16:
        block = block.astype(jnp.float32)
    return block.reshape(owners * share, width).astype(jnp.bfloat16)


def kernel(
    frames, chips, chunks,
    tokens, gain_s, w_s_in, w_so_in, gain_t, w_t_in, w_to_in,
    out,
    own, w_s, w_so, w_t, w_to, land, kv, qs, acc, peak, total, after,
    sec_out, sec_in, ctx_out, ctx_in,
    load_sem, peer_send, sib_send, land_recv, sec_send, sec_recv, ctx_send, ctx_recv,
):
    rows, width = own.shape
    half = rows // HALVES
    chunk = rows // chunks
    share = chunk // frames
    group = GROUP * HEAD
    groups = width // group
    frame = lax.axis_index("frame")
    row = lax.axis_index("row")
    core = lax.rem(row, 2)
    chip = lax.div(row, 2)
    sibling = row + 1 - 2 * core

    def chip_peer(d):
        return lax.rem(chip + d, chips) * 2 + core

    def frame_peer(d):
        return lax.rem(frame + d, frames)

    loads = [
        pltpu.make_async_copy(src, dst, load_sem.at[i])
        for i, (src, dst) in enumerate(
            [(tokens, own), (w_s_in, w_s), (w_so_in, w_so), (w_t_in, w_t), (w_to_in, w_to)]
        )
    ]
    for load in loads:
        load.start()

    barrier = pltpu.get_barrier_semaphore()

    def greet(device):
        pl.semaphore_signal(barrier, inc=1, device_id=device, device_id_type=MESH)

    greet({"row": sibling})
    loop(1, chips, lambda d: greet({"row": chip_peer(d)}))
    loop(1, frames, lambda d: greet({"frame": frame_peer(d)}))
    pl.semaphore_wait(barrier, 1 + (chips - 1) + (frames - 1))

    def to_peer(d, h):
        part = pl.ds(h * half, half)
        slot = 2 * (chips - d)
        return pltpu.make_async_remote_copy(
            src_ref=tokens.at[part], dst_ref=land.at[slot, part],
            send_sem=peer_send.at[d, h], recv_sem=land_recv.at[slot, h],
            device_id={"row": chip_peer(d)}, device_id_type=MESH,
        )

    def to_sibling(j, h):
        part = pl.ds(h * half, half)
        slot = 2 * j + 1
        src = tokens.at[part] if isinstance(j, int) and j == 0 else land.at[2 * j, part]
        return pltpu.make_async_remote_copy(
            src_ref=src, dst_ref=land.at[slot, part],
            send_sem=sib_send.at[j, h], recv_sem=land_recv.at[slot, h],
            device_id={"row": sibling}, device_id_type=MESH,
        )

    for h in range(HALVES):
        loop(1, chips, lambda d: to_peer(d, h).start())
    for h in range(HALVES):
        to_sibling(0, h).start()

    def keys_values(tokens_in, place):
        normed = layer_norm(tokens_in.astype(jnp.float32), gain_s[...]).astype(jnp.bfloat16)
        n = normed.shape[0]
        kv[pl.ds(place, n), :] = dot(normed, w_s[:, width:]).astype(jnp.bfloat16)
        return normed

    loads[0].wait()
    loads[1].wait()
    normed = keys_values(own[...], 0)
    query = dot(normed, w_s[:, :width]).astype(jnp.bfloat16)
    for c in range(chunks):
        for g in range(groups):
            qs[c, g] = stack_heads(query[c * chunk : (c + 1) * chunk, g * group : (g + 1) * group])
    for h in range(HALVES):
        to_sibling(0, h).wait_recv()
    keys_values(land[1], rows)

    def attend(c, j, first):
        place = j * (2 * rows)
        if not isinstance(j, int):
            place = pl.multiple_of(place, 2 * rows)
        for g in range(groups):
            keys = kv[pl.ds(place, 2 * rows), g * group : (g + 1) * group]
            values = kv[pl.ds(place, 2 * rows), width + g * group : width + (g + 1) * group]
            scores = dot_t(qs[c, g], keys)
            high = jnp.max(scores, axis=1, keepdims=True)
            if not first:
                before = peak[c, g][:, :1]
                high = jnp.maximum(before, high)
                fade = jnp.exp2((before - high) * FACTOR)
            weights = jnp.exp2((scores - high) * FACTOR)
            added = jnp.sum(weights, axis=1, keepdims=True)
            product = dot(weights.astype(jnp.bfloat16), values)
            if first:
                acc[c, g] = product
            else:
                added = added + total[c, g][:, :1] * fade
                acc[c, g] = acc[c, g] * fade + product
            peak[c, g] = jnp.broadcast_to(high, peak.shape[2:])
            total[c, g] = jnp.broadcast_to(added, total.shape[2:])

    for c in range(chunks):
        attend(c, 0, True)

    def take(j):
        for h in range(HALVES):
            to_peer(chips - j, h).wait_recv()
            to_sibling(j, h).start()
            keys_values(land[2 * j, pl.ds(h * half, half)], 2 * j * rows + h * half)
        for h in range(HALVES):
            to_sibling(j, h).wait_recv()
            keys_values(land[2 * j + 1, pl.ds(h * half, half)], (2 * j + 1) * rows + h * half)

    loop(1, chips, take)
    loads[2].wait()

    def exchange(c, d, src, dst, send, recv):
        peer = frame_peer(d)
        return pltpu.make_async_remote_copy(
            src_ref=src.at[c, peer], dst_ref=dst.at[c, frame],
            send_sem=send.at[c, d], recv_sem=recv.at[c, frames - d],
            device_id={"frame": peer}, device_id_type=MESH,
        )

    def second_copy(c, d):
        return exchange(c, d, sec_out, sec_in, sec_send, sec_recv)

    def context_copy(c, d):
        return exchange(c, d, ctx_out, ctx_in, ctx_send, ctx_recv)

    for c in range(chunks):
        loop(1, chips, lambda j: attend(c, j, False))
        parts = [unstack_heads(acc[c, g] / total[c, g][:, :1]) for g in range(groups)]
        context = jnp.concatenate(parts, axis=1).astype(jnp.bfloat16)
        here = slice(c * chunk, (c + 1) * chunk)
        rest = own[here].astype(jnp.float32) + dot(context, w_so[...])
        after[here] = rest
        second = layer_norm(rest, gain_t[...]).reshape(frames, share, width).astype(jnp.bfloat16)
        sec_out[c] = second
        loop(1, frames, lambda d: second_copy(c, d).start())
        sec_in[c, frame] = sec_out[c, frame]

    loads[3].wait()
    shape = (GROUP * chunk, chunk)
    q_place = lax.rem(lax.broadcasted_iota(jnp.int32, shape, 0), jnp.int32(chunk))
    k_place = lax.broadcasted_iota(jnp.int32, shape, 1)
    seen = (lax.rem(q_place, jnp.int32(share)) == lax.rem(k_place, jnp.int32(share))) & (
        k_place <= q_place
    )
    for c in range(chunks):
        loop(1, frames, lambda d: second_copy(c, d).wait_recv())
        qkv = dot(rows_of(sec_in[c]), w_t[...]).astype(jnp.bfloat16)
        parts = []
        for g in range(groups):
            query = stack_heads(qkv[:, g * group : (g + 1) * group])
            keys = qkv[:, width + g * group : width + (g + 1) * group]
            values = qkv[:, 2 * width + g * group : 2 * width + (g + 1) * group]
            scores = jnp.where(seen, dot_t(query, keys), -1e30)
            high = jnp.max(scores, axis=1, keepdims=True)
            weights = jnp.exp2((scores - high) * FACTOR)
            added = jnp.sum(weights, axis=1, keepdims=True)
            parts.append(unstack_heads(dot(weights.astype(jnp.bfloat16), values) / added))
        context = jnp.concatenate(parts, axis=1).reshape(frames, share, width)
        ctx_out[c] = context.astype(jnp.bfloat16)
        loop(1, frames, lambda d: context_copy(c, d).start())
        ctx_in[c, frame] = ctx_out[c, frame]

    loads[4].wait()
    for c in range(chunks):
        loop(1, frames, lambda d: context_copy(c, d).wait_recv())
        here = slice(c * chunk, (c + 1) * chunk)
        out[here] = (after[here] + dot(rows_of(ctx_in[c]), w_to[...])).astype(out.dtype)

    for h in range(HALVES):
        loop(1, chips, lambda d: to_peer(d, h).wait_send())
        to_sibling(0, h).wait_send()
        loop(1, chips, lambda j: to_sibling(j, h).wait_send())
    for c in range(chunks):
        loop(1, frames, lambda d: second_copy(c, d).wait_send())
        loop(1, frames, lambda d: context_copy(c, d).wait_send())


def shards(tokens, gain_s, w_s, w_so, gain_t, w_t, w_to):
    _, rows, width = tokens.shape
    frames = lax.axis_size("frame")
    peers = lax.axis_size("row")
    chips = peers // 2
    chunks = 2 if rows // frames % 32 == 0 else 1
    chunk = rows // chunks
    share = chunk // frames
    group = GROUP * HEAD
    groups = width // group
    bf16, f32 = jnp.bfloat16, jnp.float32
    vmem = pl.BlockSpec(memory_space=pltpu.VMEM)
    hbm = pl.BlockSpec(memory_space=pl.ANY)
    dma = pltpu.SemaphoreType.DMA
    mixed = pl.pallas_call(
        functools.partial(kernel, frames, chips, chunks),
        out_shape=jax.ShapeDtypeStruct((rows, width), bf16),
        in_specs=[hbm, vmem, hbm, hbm, vmem, hbm, hbm],
        out_specs=vmem,
        scratch_shapes=[
            pltpu.VMEM((rows, width), bf16),
            pltpu.VMEM(w_s.shape, bf16),
            pltpu.VMEM(w_so.shape, bf16),
            pltpu.VMEM(w_t.shape, bf16),
            pltpu.VMEM(w_to.shape, bf16),
            pltpu.VMEM((peers, rows, width), bf16),
            pltpu.VMEM((peers * rows, 2 * width), bf16),
            pltpu.VMEM((chunks, groups, GROUP * chunk, group), bf16),
            pltpu.VMEM((chunks, groups, GROUP * chunk, group), f32),
            pltpu.VMEM((chunks, groups, GROUP * chunk, 128), f32),
            pltpu.VMEM((chunks, groups, GROUP * chunk, 128), f32),
            pltpu.VMEM((rows, width), f32),
            pltpu.VMEM((chunks, frames, share, width), bf16),
            pltpu.VMEM((chunks, frames, share, width), bf16),
            pltpu.VMEM((chunks, frames, share, width), bf16),
            pltpu.VMEM((chunks, frames, share, width), bf16),
            dma((5,)),
            dma((chips, HALVES)),
            dma((chips, HALVES)),
            dma((peers, HALVES)),
            dma((chunks, frames)),
            dma((chunks, frames)),
            dma((chunks, frames)),
            dma((chunks, frames)),
        ],
        compiler_params=pltpu.CompilerParams(
            collective_id=0, has_side_effects=True, vmem_limit_bytes=52 * 1024 * 1024
        ),
        cost_estimate=pl.CostEstimate(
            flops=6_000_000_000, bytes_accessed=8_000_000, transcendentals=4_000_000
        ),
    )(tokens.reshape(rows, width), gain_s.reshape(1, width), w_s, w_so, gain_t.reshape(1, width), w_t, w_to)
    return mixed.reshape(1, rows, width)


def solution(mesh):
    in_specs = (P("frame", "row", None), P(), P(), P(), P(), P(), P())
    out_specs = P("frame", "row", None)
    return jax.shard_map(shards, mesh=mesh, in_specs=in_specs, out_specs=out_specs, check_vma=False)
```

time: 119 us -> 40.6 us (0.34)
  waiting for transfers between devices: 44.3 us -> 0 us
  Pallas kernels: 0 us -> 35.2 us
  matrix products: 21.2 us -> 0 us
  between operations: 13.6 us -> 0.01 us
  blocking collectives: 12.5 us -> 0 us
  other arithmetic: 9.17 us -> 0 us
  local copies, waits for them, and re-layouts: 12.3 us -> 5.1 us
  starting transfers between devices: 5.51 us -> 0 us
    pallas_call x0 -> x1, Pallas kernels: none -> 35.2 us  [shards(): pl.pallas_call(functools.partial(kernel, frames, chips, chunks), out_shap...]
    all_gather x1 -> x0, waiting for transfers between devices: 23.8 us -> none  [shards(): piece = lax.all_gather(pairs, 'row', axis=0, tiled=True)]
    dot_general x11 -> x0, matrix products: 21.2 us -> none  [the longest x2 5.39 us: one_block(): jnp.einsum('qhe,khe->hqk', query, key_rows, preferred_element_type=jnp.fl...]
    all_to_all x1 -> x0, waiting for transfers between devices: 20.5 us -> none  [shards(): lax.all_to_all(qkv_t, 'frame', split_axis=1, concat_axis=0, tiled=True)]
    all_to_all x1 -> x0, blocking collectives: 12.5 us -> none  [shards(): lax.all_to_all(gathered, 'frame', split_axis=0, concat_axis=1, tiled=True)]
    reduce_sum x6 -> x0, other arithmetic: 9.05 us -> none  [the longest x2 6.06 us: one_block(): total = total * fade + jnp.sum(weights, axis=2)]
    slice x4 -> x0, local copies, waits for them, and re-layouts: 7.53 us -> none  [the longest x2 5.26 us: shards(): piece[:, width:].reshape(length, HEADS, size)]
    all_to_all x1 -> x0, starting transfers between devices: 5.51 us -> none  [shards(): lax.all_to_all(qkv_t, 'frame', split_axis=1, concat_axis=0, tiled=True)]
  transfers between devices with their start and end apart: 2 -> 0, of which waited for: 2 -> 0; matrix products, arithmetic and copies ran while one was open for 1% -> 0% of each run, Pallas kernels for 0% -> 0%
where the time goes in v1:
time: 40.6 us; the launch traced here: 40.3 us
  Pallas kernels  35.2 us (87%)
  local copies, waits for them, and re-layouts  5.1 us (13%)
    pallas_call x1, Pallas kernels, shards(): pl.pallas_call(functools.partial(kernel, frames, chips, chunks), out_shap...  35.2 us
    unnamed x11, local copies, waits for them, and re-layouts  5.1 us

profile of v1, /device:TPU:0, one launch (start us, length us, event | category | flops | bytes accessed | tf_op | source)
XLA Modules:
  0.0 40.3 jit_solution(1826578830292036127)
XLA Ops:
  0.0 0.0 copy-start
  0.0 1.0 %copy-done = bf16[512,512]{1,0:T(8,128)(2,1)S(1)} copy-done((bf16[512,512]{1,0:T(8,128)(2,1)S(1)}, bf16[512,512]{1,0:T(8,128)(2,1)}, u32[]{:S(2)}) %copy-start) | copy-done | bytes 524312
  1.0 0.0 copy-start.1
  1.0 1.0 %copy-done.1 = bf16[512,512]{1,0:T(8,128)(2,1)S(1)} copy-done((bf16[512,512]{1,0:T(8,128)(2,1)S(1)}, bf16[512,512]{1,0:T(8,128)(2,1)}, u32[]{:S(2)}) %copy-start.1) | copy-done | bytes 524312
  2.1 0.0 copy-start.2
  2.1 0.9 %copy-done.2 = bf16[1,256,512]{2,1,0:T(8,128)(2,1)S(1)} copy-done((bf16[1,256,512]{2,1,0:T(8,128)(2,1)S(1)}, bf16[1,256,512]{2,1,0:T(8,128)(2,1)}, u32[]{:S(2)}) %copy-start.2) | copy-done | bytes 262168
  3.0 0.0 copy-start.3
  3.0 0.7 %copy-done.3 = f32[512]{0:T(512)S(1)} copy-done((f32[512]{0:T(512)S(1)}, f32[512]{0:T(512)}, u32[]{:S(2)}) %copy-start.3) | copy-done | bytes 2072
  3.7 0.0 copy-start.4
  3.7 0.7 %copy-done.4 = f32[512]{0:T(512)S(1)} copy-done((f32[512]{0:T(512)S(1)}, f32[512]{0:T(512)}, u32[]{:S(2)}) %copy-start.4) | copy-done | bytes 2072
  4.4 35.2 %shard_map.73 = bf16[256,512]{1,0:T(8,128)(2,1)S(1)} custom-call(bf16[256,512]{1,0:T(8,128)(2,1)S(1)} %bitcast.5, f32[1,512]{1,0:T(1,128)S(1)} %bitcast.6, bf16[512,1536]{1,0:T(8,128)(2,1)} %w_s_in.1, bf16[512,512]{1,0:T(8,128)(2,1)S(1)} %copy-done, f32[1,512]{1,0:T(1,128)S(1)} %bitcast.7, bf16[512,1536]{1,0:T(8,128)(2,1)} %w_t_in.1, ...), custom_call_target="tpu_custom_call" | custom-call | flops 6000000000 | bytes 8000000 | tf_op jit(solution)/shard_map/pallas_call | solution.py:273
  39.6 0.7 %copy.9 = bf16[1,256,512]{2,1,0:T(8,128)(2,1)} copy(bf16[1,256,512]{2,1,0:T(8,128)(2,1)S(1)} %bitcast.4) | data formatting | bytes 524288
Async XLA Ops:
  0.0 1.0 %copy-start = (bf16[512,512]{1,0:T(8,128)(2,1)S(1)}, bf16[512,512]{1,0:T(8,128)(2,1)}, u32[]{:S(2)}) copy-start(bf16[512,512]{1,0:T(8,128)(2,1)} %w_so_in.1) | copy-start | bytes 1572868
  1.0 1.0 %copy-start.1 = (bf16[512,512]{1,0:T(8,128)(2,1)S(1)}, bf16[512,512]{1,0:T(8,128)(2,1)}, u32[]{:S(2)}) copy-start(bf16[512,512]{1,0:T(8,128)(2,1)} %w_to_in.1) | copy-start | bytes 1572868
  2.1 0.9 %copy-start.2 = (bf16[1,256,512]{2,1,0:T(8,128)(2,1)S(1)}, bf16[1,256,512]{2,1,0:T(8,128)(2,1)}, u32[]{:S(2)}) copy-start(bf16[1,256,512]{2,1,0:T(8,128)(2,1)} %param.7) | copy-start | bytes 786436
  3.0 0.7 %copy-start.3 = (f32[512]{0:T(512)S(1)}, f32[512]{0:T(512)}, u32[]{:S(2)}) copy-start(f32[512]{0:T(512)} %param.8) | copy-start | bytes 6148
  3.7 0.7 %copy-start.4 = (f32[512]{0:T(512)S(1)}, f32[512]{0:T(512)}, u32[]{:S(2)}) copy-start(f32[512]{0:T(512)} %param.11) | copy-start | bytes 6148

commit v2 on v1

--- a/solution.py
+++ b/solution.py
@@ -10,6 +10,7 @@
 
 HEADS = 8
 HEAD = 64
+LANES = 128
 GROUP = 4
 HALVES = 2
 FACTOR = math.log2(math.e) / math.sqrt(HEAD)
@@ -51,7 +52,7 @@
 
 
 def loop(low, high, body):
-    if high - low <= 1:
+    if high - low <= 8:
         for i in range(low, high):
             body(i)
     else:
@@ -151,43 +152,53 @@
         to_sibling(0, h).wait_recv()
     keys_values(land[1], rows)
 
-    def attend(c, j, first):
-        place = j * (2 * rows)
-        if not isinstance(j, int):
-            place = pl.multiple_of(place, 2 * rows)
+    def attend(c, place, count, first=False):
+        if not isinstance(place, int):
+            place = pl.multiple_of(place, count)
         for g in range(groups):
-            keys = kv[pl.ds(place, 2 * rows), g * group : (g + 1) * group]
-            values = kv[pl.ds(place, 2 * rows), width + g * group : width + (g + 1) * group]
+            keys = kv[pl.ds(place, count), g * group : (g + 1) * group]
+            values = kv[pl.ds(place, count), width + g * group : width + (g + 1) * group]
             scores = dot_t(qs[c, g], keys)
             high = jnp.max(scores, axis=1, keepdims=True)
             if not first:
-                before = peak[c, g][:, :1]
-                high = jnp.maximum(before, high)
-                fade = jnp.exp2((before - high) * FACTOR)
+                before = peak[c, g]
+                high = jnp.maximum(before[:, :1], high)
             weights = jnp.exp2((scores - high) * FACTOR)
-            added = jnp.sum(weights, axis=1, keepdims=True)
+            added = sum(weights[:, i : i + LANES] for i in range(0, count, LANES))
             product = dot(weights.astype(jnp.bfloat16), values)
+            high = jnp.broadcast_to(high, peak.shape[2:])
             if first:
                 acc[c, g] = product
+                total[c, g] = added
             else:
-                added = added + total[c, g][:, :1] * fade
-                acc[c, g] = acc[c, g] * fade + product
-            peak[c, g] = jnp.broadcast_to(high, peak.shape[2:])
-            total[c, g] = jnp.broadcast_to(added, total.shape[2:])
-
-    for c in range(chunks):
-        attend(c, 0, True)
-
-    def take(j):
-        for h in range(HALVES):
-            to_peer(chips - j, h).wait_recv()
-            to_sibling(j, h).start()
-            keys_values(land[2 * j, pl.ds(h * half, half)], 2 * j * rows + h * half)
-        for h in range(HALVES):
-            to_sibling(j, h).wait_recv()
-            keys_values(land[2 * j + 1, pl.ds(h * half, half)], (2 * j + 1) * rows + h * half)
-
-    loop(1, chips, take)
+                fade = jnp.exp2((before - high) * FACTOR)
+                total[c, g] = total[c, g] * fade + added
+                acc[c, g] = acc[c, g] * jnp.concatenate([fade] * (group // LANES), 1) + product
+            peak[c, g] = high
+
+    for c in range(chunks):
+        attend(c, 0, 2 * rows, True)
+
+    def place_of(j, h):
+        return 2 * j * rows + h * 2 * half
+
+    def take(j, h):
+        part = pl.ds(h * half, half)
+        to_peer(chips - j, h).wait_recv()
+        to_sibling(j, h).start()
+        keys_values(land[2 * j, part], place_of(j, h))
+        to_sibling(j, h).wait_recv()
+        keys_values(land[2 * j + 1, part], place_of(j, h) + half)
+
+    def take_and_attend(j, h):
+        take(j, h)
+        for c in range(chunks):
+            attend(c, place_of(j, h), 2 * half)
+
+    last = HALVES - 1
+    for h in range(last):
+        loop(1, chips, lambda j: take_and_attend(j, h))
+    loop(1, chips, lambda j: take(j, last))
     loads[2].wait()
 
     def exchange(c, d, src, dst, send, recv):
@@ -198,6 +209,9 @@
             device_id={"frame": peer}, device_id_type=MESH,
         )
 
+    def far_first(i):
+        return frames // 2 + (i // 2) * (1 - 2 * (i % 2))
+
     def second_copy(c, d):
         return exchange(c, d, sec_out, sec_in, sec_send, sec_recv)
 
@@ -205,15 +219,18 @@
         return exchange(c, d, ctx_out, ctx_in, ctx_send, ctx_recv)
 
     for c in range(chunks):
-        loop(1, chips, lambda j: attend(c, j, False))
-        parts = [unstack_heads(acc[c, g] / total[c, g][:, :1]) for g in range(groups)]
+        loop(1, chips, lambda j: attend(c, place_of(j, last), 2 * half))
+        parts = [
+            unstack_heads(acc[c, g] / jnp.sum(total[c, g], axis=1, keepdims=True))
+            for g in range(groups)
+        ]
         context = jnp.concatenate(parts, axis=1).astype(jnp.bfloat16)
         here = slice(c * chunk, (c + 1) * chunk)
         rest = own[here].astype(jnp.float32) + dot(context, w_so[...])
         after[here] = rest
         second = layer_norm(rest, gain_t[...]).reshape(frames, share, width).astype(jnp.bfloat16)
         sec_out[c] = second
-        loop(1, frames, lambda d: second_copy(c, d).start())
+        loop(1, frames, lambda i: second_copy(c, far_first(i)).start())
         sec_in[c, frame] = sec_out[c, frame]
 
     loads[3].wait()
@@ -238,7 +255,7 @@
             parts.append(unstack_heads(dot(weights.astype(jnp.bfloat16), values) / added))
         context = jnp.concatenate(parts, axis=1).reshape(frames, share, width)
         ctx_out[c] = context.astype(jnp.bfloat16)
-        loop(1, frames, lambda d: context_copy(c, d).start())
+        loop(1, frames, lambda i: context_copy(c, far_first(i)).start())
         ctx_in[c, frame] = ctx_out[c, frame]
 
     loads[4].wait()
@@ -285,8 +302,8 @@
             pltpu.VMEM((peers * rows, 2 * width), bf16),
             pltpu.VMEM((chunks, groups, GROUP * chunk, group), bf16),
             pltpu.VMEM((chunks, groups, GROUP * chunk, group), f32),
-            pltpu.VMEM((chunks, groups, GROUP * chunk, 128), f32),
-            pltpu.VMEM((chunks, groups, GROUP * chunk, 128), f32),
+            pltpu.VMEM((chunks, groups, GROUP * chunk, LANES), f32),
+            pltpu.VMEM((chunks, groups, GROUP * chunk, LANES), f32),
             pltpu.VMEM((rows, width), f32),
             pltpu.VMEM((chunks, frames, share, width), bf16),
             pltpu.VMEM((chunks, frames, share, width), bf16),
@@ -302,7 +319,7 @@
             dma((chunks, frames)),
         ],
         compiler_params=pltpu.CompilerParams(
-            collective_id=0, has_side_effects=True, vmem_limit_bytes=52 * 1024 * 1024
+            collective_id=0, has_side_effects=True, vmem_limit_bytes=64 * 1024 * 1024
         ),
         cost_estimate=pl.CostEstimate(
             flops=6_000_000_000, bytes_accessed=8_000_000, transcendentals=4_000_000

time: 40.6 us -> 37.7 us (0.929)
  local copies, waits for them, and re-layouts: 5.1 us -> 1.67 us
  Pallas kernels: 35.2 us -> 35.8 us
    unnamed x11 -> x1, local copies, waits for them, and re-layouts: 5.1 us -> 1.67 us
    pallas_call x1, Pallas kernels: 35.2 us -> 35.8 us  [shards(): pl.pallas_call(functools.partial(kernel, frames, chips, chunks), out_shap...]
where the time goes in v2:
time: 37.7 us; the launch traced here: 37.5 us
  Pallas kernels  35.8 us (95%)
  local copies, waits for them, and re-layouts  1.67 us (4%)
    pallas_call x1, Pallas kernels, shards(): pl.pallas_call(functools.partial(kernel, frames, chips, chunks), out_shap...  35.8 us
    unnamed x1, local copies, waits for them, and re-layouts  1.67 us

profile of v2, /device:TPU:0, one launch (start us, length us, event | category | flops | bytes accessed | tf_op | source)
XLA Modules:
  0.0 37.5 jit_solution(1667310603566830746)
XLA Ops:
  0.0 35.8 %shard_map.73 = bf16[256,512]{1,0:T(8,128)(2,1)} custom-call(bf16[256,512]{1,0:T(8,128)(2,1)} %bitcast.5, f32[1,512]{1,0:T(1,128)} %bitcast.6, bf16[512,1536]{1,0:T(8,128)(2,1)} %w_s_in.1, bf16[512,512]{1,0:T(8,128)(2,1)} %w_so_in.1, f32[1,512]{1,0:T(1,128)} %bitcast.7, bf16[512,1536]{1,0:T(8,128)(2,1)} %w_t_in.1, bf16[512,512]{1,0:T(8,128)(2,1)} %w_to_in.1), custom_call_target="tpu_custom_call" | custom-call | flops 6000000000 | bytes 8000000 | tf_op jit(solution)/shard_map/pallas_call | solution.py:290
  35.8 1.7 %copy.9 = bf16[1,256,512]{2,1,0:T(8,128)(2,1)} copy(bf16[1,256,512]{2,1,0:T(8,128)(2,1)} %bitcast.4) | data formatting | bytes 524288

commit v3 on v2

--- a/solution.py
+++ b/solution.py
@@ -221,7 +221,7 @@
     for c in range(chunks):
         loop(1, chips, lambda j: attend(c, place_of(j, last), 2 * half))
         parts = [
-            unstack_heads(acc[c, g] / jnp.sum(total[c, g], axis=1, keepdims=True))
+            unstack_heads(acc[c, g] * (1.0 / jnp.sum(total[c, g], axis=1, keepdims=True)))
             for g in range(groups)
         ]
         context = jnp.concatenate(parts, axis=1).astype(jnp.bfloat16)
@@ -252,7 +252,7 @@
             high = jnp.max(scores, axis=1, keepdims=True)
             weights = jnp.exp2((scores - high) * FACTOR)
             added = jnp.sum(weights, axis=1, keepdims=True)
-            parts.append(unstack_heads(dot(weights.astype(jnp.bfloat16), values) / added))
+            parts.append(unstack_heads(dot(weights.astype(jnp.bfloat16), values) * (1.0 / added)))
         context = jnp.concatenate(parts, axis=1).reshape(frames, share, width)
         ctx_out[c] = context.astype(jnp.bfloat16)
         loop(1, frames, lambda i: context_copy(c, far_first(i)).start())
@@ -289,7 +289,7 @@
     dma = pltpu.SemaphoreType.DMA
     mixed = pl.pallas_call(
         functools.partial(kernel, frames, chips, chunks),
-        out_shape=jax.ShapeDtypeStruct((rows, width), bf16),
+        out_shape=pltpu.VMEM((rows, width), bf16),
         in_specs=[hbm, vmem, hbm, hbm, vmem, hbm, hbm],
         out_specs=vmem,
         scratch_shapes=[
@@ -319,7 +319,7 @@
             dma((chunks, frames)),
         ],
         compiler_params=pltpu.CompilerParams(
-            collective_id=0, has_side_effects=True, vmem_limit_bytes=64 * 1024 * 1024
+            collective_id=0, has_side_effects=True, vmem_limit_bytes=63 * 1024 * 1024
         ),
         cost_estimate=pl.CostEstimate(
             flops=6_000_000_000, bytes_accessed=8_000_000, transcendentals=4_000_000

time: 37.7 us -> 36 us (0.955)
  local copies, waits for them, and re-layouts: 1.67 us -> 0.71 us
  Pallas kernels: 35.8 us -> 35.2 us
    unnamed x1, local copies, waits for them, and re-layouts: 1.67 us -> 0.71 us
    pallas_call x1, Pallas kernels: 35.8 us -> 35.2 us  [shards(): pl.pallas_call(functools.partial(kernel, frames, chips, chunks), out_shap...]
where the time goes in v3:
time: 36 us; the launch traced here: 35.9 us
  Pallas kernels  35.2 us (98%)
  local copies, waits for them, and re-layouts  0.71 us (2%)
    pallas_call x1, Pallas kernels, shards(): pl.pallas_call(functools.partial(kernel, frames, chips, chunks), out_shap...  35.2 us

profile of v3, /device:TPU:0, one launch (start us, length us, event | category | flops | bytes accessed | tf_op | source)
XLA Modules:
  0.0 35.9 jit_solution(12412075677864106774)
XLA Ops:
  0.0 35.2 %shard_map.73 = bf16[256,512]{1,0:T(8,128)(2,1)S(1)} custom-call(bf16[256,512]{1,0:T(8,128)(2,1)} %bitcast.5, f32[1,512]{1,0:T(1,128)} %bitcast.6, bf16[512,1536]{1,0:T(8,128)(2,1)} %w_s_in.1, bf16[512,512]{1,0:T(8,128)(2,1)} %w_so_in.1, f32[1,512]{1,0:T(1,128)} %bitcast.7, bf16[512,1536]{1,0:T(8,128)(2,1)} %w_t_in.1, bf16[512,512]{1,0:T(8,128)(2,1)} %w_to_in.1), custom_call_target="tpu_custom_call" | custom-call | flops 6000000000 | bytes 8000000 | tf_op jit(solution)/shard_map/pallas_call | solution.py:290
  35.2 0.7 %copy.9 = bf16[1,256,512]{2,1,0:T(8,128)(2,1)} copy(bf16[1,256,512]{2,1,0:T(8,128)(2,1)S(1)} %bitcast.4) | data formatting | bytes 524288
